TPU v7x, 128 devices: a whole 4x4x4 slice. The times are simulated.
128 devices in a mesh: lat: 4 (over z_lo, core), lon: 32 (over y, x, z_hi).
Axes of the slice: x: 4, y: 4, z: 4 (z_hi: 2, z_lo: 2; z = z_hi * 2 + z_lo), core: 2. Of those that a mesh axis runs over, the one named last changes fastest.
Arguments:
- lattice_site_embedding: bfloat16 [512, 256, 768], P('lat', 'lon'), may hold values from -24 to 24
- final_lattice_sensitivity: bfloat16 [512, 256, 768], P('lat', 'lon'), may hold values from -6 to 6
- patch_rescale_coeffs: float32 [768], replicated, may hold values from 0.25 to 1.75
- patch_triple_linear: bfloat16 [768, 2304], replicated, may hold values from -0.21875 to 0.21875
- patch_exit_linear: bfloat16 [768, 768], replicated, may hold values from -0.21875 to 0.21875
- patch_logit_temper: float32 [12], replicated, may hold values from 2 to 25
- bearer_rescale_coeffs: float32 [768], replicated, may hold values from 0.25 to 1.75
- bearer_triple_linear: bfloat16 [768, 2304], replicated, may hold values from -0.21875 to 0.21875
- bearer_exit_linear: bfloat16 [768, 768], replicated, may hold values from -0.21875 to 0.21875
- bearer_logit_temper: float32 [12], replicated, may hold values from 2 to 25
- bearer_sequence_place: int32 [128, 64], P('lat', 'lon'), may hold values from 0 to 2047, as said below
Outputs:
- out_field: bfloat16 [512, 256, 768], P('lat', 'lon')
- field_grad: bfloat16 [512, 256, 768], P('lat', 'lon')
Inputs may be any that keep to these rules, and one draw needn't show every extreme that they name: `bearer_sequence_place`: places within one row of devices (the carriers of 128 grid rows) are all different. Of the 64 carriers of one device, exactly 2 have place // 64 equal to each lon index, and for these (place % 64) // 2 is the lon index of the device that holds the carrier.
All inputs are finite; a program needn't handle non-finite values.
Results may differ from a plain program's by a relative error of at most 0.014.
Values may be sent and summed in bfloat16 or wider, within the bound.
A program may use at most 192 MiB of HBM per device.

v0:
```python
import types

import jax
import jax.numpy as jnp
from jax import lax
from jax.experimental import pallas as pl
from jax.experimental.pallas import tpu as pltpu
from jax.sharding import PartitionSpec as P

BF = jnp.bfloat16
F32 = jnp.float32
LOG2E = 1.4426950408889634
LN2 = 0.6931471805599453
D = 768
GROUPS = 3
WINDOWS = 16
CELLS = 64
HALF = 512
MESH = pl.DeviceIdType.MESH


def nn(a, b):
    return lax.dot_general(a, b, (((1,), (0,)), ((), ())), preferred_element_type=F32)


def nt(a, b):
    return lax.dot_general(a, b, (((1,), (1,)), ((), ())), preferred_element_type=F32)


def tn(a, b):
    return lax.dot_general(a, b, (((0,), (0,)), ((), ())), preferred_element_type=F32)


def iota(shape, axis):
    return lax.broadcasted_iota(jnp.int32, shape, axis)


def one_where(condition):
    return jnp.where(condition, 1.0, 0.0).astype(BF)


def lanes(n):
    return slice(n * 256, (n + 1) * 256)


def fill_constants(k):
    k.heads[...] = one_where(iota((256, 256), 0) // 64 == iota((256, 256), 1) // 64)
    k.carrier_heads[...] = one_where(iota((256, D), 0) % 16 == iota((256, D), 1) // 64)
    k.same[...] = one_where(iota((256, 256), 0) % 128 // 32 == iota((256, 256), 1) % 128 // 32)
    k.spread[...] = one_where(iota((1024, 64), 0) // 16 == iota((1024, 64), 1))
    k.gather[...] = one_where(iota((64, 1024), 1) // 16 == iota((64, 1024), 0))
    split, cell = iota((256, 256), 0), iota((256, 256), 1)
    k.split[...] = one_where(cell == split % 128 // 4 * 8 + split // 128 * 4 + split % 4)
    row, slab = iota((384, HALF), 0), iota((384, HALF), 1)
    member = row % 64
    k.unpack[...] = one_where(slab == member // 2 * 16 + row // 64 * 2 + member % 2)
    k.gain[...] = k.gains[...].reshape(1, D)
    k.cgain[...] = k.cgains[...].reshape(1, D)
    lane = iota((1, D), 1) // 64
    for tempers, wide in ((k.tempers, k.temper), (k.ctempers, k.ctemper)):
        total = jnp.zeros((1, D), F32)
        for h in range(12):
            total = jnp.where(lane == h, tempers[h], total)
        wide[...] = total


def fill_routes(k, lon):
    slab = iota((32, HALF), 1)
    eye = jnp.where(iota((32, 32), 0) == iota((32, 32), 1), 1.0, 0.0)
    for b in range(2):
        place = k.place[b : b + 1, :]
        place = jnp.sum(jnp.where(eye > 0, place, 0), axis=1, keepdims=True)
        partner = (place // 64 - lon + 32) % 32
        slot = partner * 16 + place % 2
        for c in range(6):
            rows = slice(b * 192 + c * 32, b * 192 + c * 32 + 32)
            k.routes[rows, :] = one_where(slab == slot + 2 * c)


def pack(matrix, parts):
    return tn(matrix, jnp.concatenate(parts, axis=0)).astype(BF).reshape(32, 16, 128)


def lane_parts(rows):
    return [rows[:, c * 128 : (c + 1) * 128] for c in range(6)]


def pack_home(k, rows):
    return pack(k.routes[...], lane_parts(rows[:32]) + lane_parts(rows[32:]))


def unpack_home(k, slabs):
    parts = nn(k.routes[...], slabs[...].reshape(HALF, 128)).astype(BF)
    sides = []
    for b in range(2):
        pieces = [parts[b * 192 + c * 32 : b * 192 + c * 32 + 32] for c in range(6)]
        sides.append(jnp.concatenate(pieces, axis=1))
    return jnp.concatenate(sides, axis=0)


def pack_owner(k, rows):
    return pack(k.unpack[...], lane_parts(rows))


def unpack_owner(k, slabs):
    parts = nn(k.unpack[...], slabs[...].reshape(HALF, 128)).astype(BF)
    return jnp.concatenate([parts[c * 64 : c * 64 + 64] for c in range(6)], axis=1)


def rms_inverse(x):
    return lax.rsqrt(jnp.mean(x * x, axis=-1, keepdims=True) + 1e-05)


def rms_back(x, gain, grad):
    inverse = rms_inverse(x)
    scaled = grad * gain
    along = jnp.mean(x * scaled, axis=-1, keepdims=True)
    return inverse * (scaled - x * (inverse * inverse * along))


def unit_scale(u, heads):
    return lax.rsqrt(nn((u * u).astype(BF), heads) + 64e-06)


def key_back(scale, key, grad, heads):
    along = nn((key * grad).astype(BF), heads)
    return scale * (grad - key * along)


def query_back(scale, query, temper, raw, heads):
    along = nn((query * raw).astype(BF), heads)
    return scale * (temper * raw - query * along * (LN2 * LN2 / temper))


def block_diagonal(rows, heads):
    return jnp.concatenate([rows] * 4, axis=0) * heads


def chunk_rows(chunk):
    return pl.ds(pl.multiple_of(chunk * 256, 256), 256)


def both(ref, quad, columns=slice(None)):
    first = pl.multiple_of(quad * 128, 128)
    return jnp.concatenate(
        [ref[pl.ds(first, 128), columns], ref[pl.ds(first + HALF, 128), columns]], axis=0
    )


def put_both(ref, quad, value, columns=slice(None)):
    first = pl.multiple_of(quad * 128, 128)
    ref[pl.ds(first, 128), columns] = value[:128]
    ref[pl.ds(first + HALF, 128), columns] = value[128:]


def window(rows, w):
    return jnp.concatenate([rows[w * 32 : w * 32 + 32], rows[w * 32 + 128 : w * 32 + 160]], axis=0)


def from_parts(parts):
    return jnp.concatenate([p[:32] for p in parts] + [p[32:] for p in parts], axis=0)


def cells_project(k, chunk):
    rows = chunk_rows(chunk)
    x = k.x[rows, :].astype(F32)
    hidden = (x * rms_inverse(x) * k.gain[...]).astype(BF)
    heads = k.heads[...]
    for n in range(GROUPS):
        u = nn(hidden, k.w[:, lanes(n)])
        scale = unit_scale(u, heads)
        k.sq[rows, lanes(n)] = scale
        k.q[rows, lanes(n)] = (u * scale * (k.temper[:, lanes(n)] * LOG2E)).astype(BF)
    for n in range(GROUPS):
        u = nn(hidden, k.w[:, lanes(3 + n)])
        scale = unit_scale(u, heads)
        k.sk[rows, lanes(n)] = scale
        k.k[rows, lanes(n)] = (u * scale).astype(BF)
    for n in range(GROUPS):
        k.v[rows, lanes(n)] = nn(hidden, k.w[:, lanes(6 + n)]).astype(BF)


def cells_sensitivity(k, quad):
    halves = nn(k.split[...], k.graw[chunk_rows(quad), :]).astype(BF)
    put_both(k.g, quad, halves)
    put_both(k.do, quad, nt(halves, k.we[...]).astype(BF))


def cells_attend(k, quad):
    heads = k.heads[...]
    for n in range(GROUPS):
        query, key, value = (both(ref, quad, lanes(n)) for ref in (k.q, k.k, k.v))
        weights, sums = [], []
        for w in range(4):
            keys = block_diagonal(window(key, w), heads)
            weights.append(jnp.exp2(nt(window(query, w), keys)).astype(BF))
        for w in range(4):
            sums.append(nn(weights[w], block_diagonal(window(value, w), heads)))
        weights = from_parts(weights)
        put_both(k.p, quad, weights, lanes(n))
        put_both(k.op, quad, from_parts(sums), lanes(n))
        put_both(k.lp, quad, nn(weights, heads), lanes(n))


def carriers_project(k):
    c = k.cn[...].astype(F32)
    hidden = (c * rms_inverse(c) * k.gain[...]).astype(BF)
    heads = k.heads[...]
    for n in range(GROUPS):
        u = nn(hidden, k.w[:, lanes(3 + n)])
        scale = unit_scale(u, heads)
        k.skc[:, lanes(n)] = scale
        key = (u * scale).astype(BF)
        k.kc[:, lanes(n)] = key
        value = nn(hidden, k.w[:, lanes(6 + n)]).astype(BF)
        k.vc[:, lanes(n)] = value
    for chunk in range(4):
        rows = slice(chunk * 256, (chunk + 1) * 256)
        mask = k.carrier_heads[...]
        k.kcb[rows, :] = nn(k.spread[rows, :], k.kc[...]).astype(BF) * mask
        k.vcb[rows, :] = nn(k.spread[rows, :], k.vc[...]).astype(BF) * mask


def windows_finish(k, quad):
    keys, values, query = both(k.kcb, quad), both(k.vcb, quad), both(k.q, quad)
    mask = k.carrier_heads[...]
    weights = jnp.exp2(nt(query, keys)).astype(BF) * k.same[...]
    along = jnp.zeros((256, 256), F32)
    for n in range(GROUPS):
        inverse = 1.0 / (both(k.lp, quad, lanes(n)) + nn(weights, mask[:, lanes(n)]))
        attended = both(k.op, quad, lanes(n)) + nn(weights, values[:, lanes(n)])
        attended = attended * inverse
        put_both(k.o, quad, attended.astype(BF), lanes(n))
        sensitivity = both(k.do, quad, lanes(n)).astype(F32) * inverse
        product = (sensitivity * attended).astype(BF)
        put_both(k.t, quad, product, lanes(n))
        sensitivity = sensitivity.astype(BF)
        put_both(k.do, quad, sensitivity, lanes(n))
        along += nt(sensitivity, values[:, lanes(n)]) - nt(product, mask[:, lanes(n)])
    grads = (weights.astype(F32) * along).astype(BF)
    put_both(k.cg, quad, grads)
    put_both(k.dqkv, quad, (tn(grads, query) * LN2).astype(BF) * mask, slice(0, D))
    put_both(k.dqkv, quad, tn(weights, both(k.do, quad)).astype(BF) * mask, slice(D, 2 * D))


def carriers_back(k):
    heads = k.heads[...]
    select = k.gather[...]
    grad = jnp.zeros((64, D), F32)
    for n in range(GROUPS):
        dk = nn(select, k.dqkv[:, lanes(n)])
        du = key_back(k.skc[:, lanes(n)], k.kc[:, lanes(n)].astype(F32), dk, heads)
        grad += nt(du.astype(BF), k.w[:, lanes(3 + n)])
        dv = nn(select, k.dqkv[:, lanes(3 + n)]).astype(BF)
        grad += nt(dv, k.w[:, lanes(6 + n)])
    grad = grad.astype(BF).astype(F32)
    back = rms_back(k.cn[...].astype(F32), k.gain[...], grad)
    return (back + k.gsum[...]).astype(BF)


def cells_result(k, quad):
    total = both(k.x, quad).astype(F32) + nn(both(k.o, quad), k.we[...])
    put_both(k.xraw, quad, (total + nn(both(k.spread, quad), k.cn[...])).astype(BF))


def cells_back(k, quad):
    heads = k.heads[...]
    low = iota((64, 128), 1) < 64
    for n in range(GROUPS):
        query, key, value = (both(ref, quad, lanes(n)) for ref in (k.q, k.k, k.v))
        weights, sensitivity = (both(ref, quad, lanes(n)) for ref in (k.p, k.do))
        offset = nn(both(k.t, quad, lanes(n)), heads)
        along = []
        for w in range(4):
            values = block_diagonal(window(value, w), heads)
            along.append(nt(window(sensitivity, w), values))
        grads = (weights.astype(F32) * (from_parts(along) - offset)).astype(BF)
        raw, dk, dv = [], [], []
        for w in range(4):
            mine = window(grads, w)
            raw.append(nn(mine, block_diagonal(window(key, w), heads)))
            key_parts, value_parts = [], []
            for pair in range(2):
                part = slice(pair * 128, (pair + 1) * 128)
                pairs = tn(mine[:, part], window(query, w)[:, part])
                key_parts.append(jnp.where(low, pairs[:64], pairs[64:]))
                pairs = tn(window(weights, w)[:, part], window(sensitivity, w)[:, part])
                value_parts.append(jnp.where(low, pairs[:64], pairs[64:]))
            dk.append(jnp.concatenate(key_parts, axis=1))
            dv.append(jnp.concatenate(value_parts, axis=1))
        put_both(k.dqkv, quad, from_parts(dv).astype(BF), lanes(6 + n))
        raw = nn(both(k.cg, quad), both(k.kcb, quad, lanes(n))) + from_parts(raw)
        scale = both(k.sq, quad, lanes(n))
        du = query_back(scale, query.astype(F32), k.temper[:, lanes(n)], raw, heads)
        put_both(k.dqkv, quad, du.astype(BF), lanes(n))
        dk = (from_parts(dk) * LN2).astype(BF).astype(F32)
        du = key_back(both(k.sk, quad, lanes(n)), key.astype(F32), dk, heads)
        put_both(k.dqkv, quad, du.astype(BF), lanes(3 + n))


def cells_gradient(k, first, count):
    rows = pl.ds(pl.multiple_of(first, 128), count)
    grad = nt(k.dqkv[rows, :], k.w[...]).astype(BF).astype(F32)
    back = rms_back(k.x[rows, :].astype(F32), k.gain[...], grad)
    k.dx[rows, :] = (back + k.g[rows, :].astype(F32)).astype(BF)


def pick(full):
    head = iota((64, 256), 1) // 64
    picked = full[:64]
    for h in range(1, 4):
        picked = jnp.where(head == h, full[h * 64 : h * 64 + 64], picked)
    return picked


def group_query(k, rows, n):
    u = nn(k.chid[rows, :], k.cw[:, lanes(n)])
    scale = unit_scale(u, k.heads[...])
    query = (u * scale * (k.ctemper[:, lanes(n)] * LOG2E)).astype(BF)
    k.cq[rows, lanes(n)] = query
    return query, scale


def group_forward(k):
    c = k.car[...].astype(F32)
    hidden = (c * rms_inverse(c) * k.cgain[...]).astype(BF)
    k.chid[...] = hidden
    heads = k.heads[...]
    ones = jnp.ones((256, 256), BF)
    for n in range(GROUPS):
        query, scale = group_query(k, slice(0, 64), n)
        k.csq[:, lanes(n)] = scale
        u = nn(hidden, k.cw[:, lanes(3 + n)])
        scale = unit_scale(u, heads)
        k.csk[:, lanes(n)] = scale[:64]
        key = (u * scale).astype(BF)
        k.ck[:, lanes(n)] = key
        value = nn(hidden, k.cw[:, lanes(6 + n)]).astype(BF)
        k.cv[:, lanes(n)] = value
        weights = jnp.exp2(nt(block_diagonal(query, heads), key)).astype(BF)
        k.crows[n] = weights
        inverse = 1.0 / nn(weights, ones)
        k.cl[:64, lanes(n)] = pick(inverse)
        k.co[:64, lanes(n)] = pick(nn(weights, value) * inverse)
    mixed = nn(k.co[:64, :].astype(BF), k.cwe[...])
    return (k.car[:64, :].astype(F32) + mixed).astype(BF)


def group_others(k):
    heads = k.heads[...]
    rows = slice(64, 256)
    for n in range(GROUPS):
        query, _ = group_query(k, rows, n)
        key, value = k.ck[:, lanes(n)], k.cv[:, lanes(n)]
        total = jnp.zeros((192, 256), F32)
        denominator = jnp.zeros((192, 256), F32)
        for h in range(4):
            mine = one_where(iota((256, 256), 1) // 64 == h)
            weights = jnp.exp2(nt(query, key * mine)).astype(BF)
            total += nn(weights, value * mine)
            denominator += nn(weights, mine)
        inverse = 1.0 / denominator
        k.cl[rows, lanes(n)] = inverse
        k.co[rows, lanes(n)] = total * inverse
        own = block_diagonal(key[:64], heads)
        k.ccolumns[n] = jnp.exp2(nt(own, k.cq[:, lanes(n)])).astype(BF)


def group_back(k):
    heads = k.heads[...]
    ones = jnp.ones((256, 256), BF)
    grad = jnp.zeros((64, D), F32)
    for n in range(GROUPS):
        sensitivity = nt(k.cgrad[...], k.cwe[lanes(n), :]).astype(BF).astype(F32)
        sensitivity = sensitivity * k.cl[:, lanes(n)]
        product = (sensitivity * k.co[:, lanes(n)]).astype(BF)
        sensitivity = sensitivity.astype(BF)
        query, key, value = k.cq[:, lanes(n)], k.ck[:, lanes(n)], k.cv[:, lanes(n)]
        along = nt(block_diagonal(sensitivity[:64], heads), value)
        along -= nn(block_diagonal(product[:64], heads), ones)
        grads = (k.crows[n].astype(F32) * along).astype(BF)
        raw = pick(nn(grads, key))
        du = query_back(
            k.csq[:, lanes(n)], query[:64].astype(F32), k.ctemper[:, lanes(n)], raw, heads
        )
        grad += nt(du.astype(BF), k.cw[:, lanes(n)])
        weights = k.ccolumns[n]
        along = nt(block_diagonal(value[:64], heads), sensitivity) - nt(heads, product)
        grads = (weights.astype(F32) * along).astype(BF)
        dk = (pick(nn(grads, query)) * LN2).astype(BF).astype(F32)
        du = key_back(k.csk[:, lanes(n)], key[:64].astype(F32), dk, heads)
        grad += nt(du.astype(BF), k.cw[:, lanes(3 + n)])
        dv = pick(nn(weights, sensitivity)).astype(BF)
        grad += nt(dv, k.cw[:, lanes(6 + n)])
    grad = grad.astype(BF).astype(F32)
    back = rms_back(k.car[:64, :].astype(F32), k.cgain[...], grad)
    return (back + k.cgrad[:64, :].astype(F32)).astype(BF)


def cells_split(k, quad):
    halves = nn(k.split[...], k.xraw[chunk_rows(quad), :]).astype(BF)
    first = quad * 128
    k.away[first : first + 128, :] = halves[:128]
    if quad == 0:
        k.rise[...] = halves[128:144]
        k.x[0:112, :] = halves[144:]
    else:
        k.x[first - 16 : first + 112, :] = halves[128:]
    means = nn(one_where(iota((16, 256), 1) // 16 == iota((16, 256), 0)), halves) * 0.0625
    k.means[0, quad * 8 : quad * 8 + 8, :] = means[:8]
    k.means[1, quad * 8 : quad * 8 + 8, :] = means[8:]


def assemble(result, grads, edges, out, field):
    cell, split = iota((256, 256), 0), iota((256, 256), 1)
    join = one_where(cell == split % 128 // 4 * 8 + split // 128 * 4 + split % 4)
    for part in range(2):
        rows, cells = slice(part * 128, part * 128 + 128), slice(part * 256, part * 256 + 256)
        group = iota((128, 32), 0) // 16 + (pl.program_id(0) * 2 + part) * 8
        out[cells, :] = nn(join, result[:, rows, :].reshape(256, D)).astype(BF)
        mine = one_where(group - 1 == iota((128, 32), 1))
        edge = one_where((group[:, :16] == 0) & (iota((128, 16), 1) == 15))
        left = nn(mine, edges[64:96, :]) + nn(edge, edges[96:112, :])
        right = nn(mine, edges[0:32, :]) + nn(edge, edges[112:128, :])
        total = grads[:, rows, :].reshape(256, D).astype(F32)
        total += jnp.concatenate([left, right], axis=0) * 0.0625
        field[cells, :] = nn(join, total.astype(BF)).astype(BF)


def body(k):
    lat, lon = lax.axis_index("lat"), lax.axis_index("lon")
    has_above, has_below = lat > 0, lat < 3
    above, below = lax.rem(lat + 3, 4), lax.rem(lat + 1, 4)
    west, east = lax.rem(lon + 31, 32), lax.rem(lon + 1, 32)

    loads = []
    for i, (source, target) in enumerate(
        (
            (k.x_hbm, k.xraw),
            (k.w_hbm, k.w),
            (k.g_hbm, k.graw),
            (k.we_hbm, k.we),
            (k.cw_hbm, k.cw),
            (k.cwe_hbm, k.cwe),
        )
    ):
        load = pltpu.make_async_copy(source, target, k.load_sem.at[i])
        load.start()
        loads.append(load)
    load_x, load_w, load_g, load_we, load_cw, load_cwe = loads

    @pl.when(jnp.logical_not(has_below))
    def _():
        k.x[496:512, :] = jnp.zeros((16, D), BF)
        k.x[1008:1024, :] = jnp.zeros((16, D), BF)
        k.car_below[...] = jnp.zeros((16, D), BF)
        k.car_corner[...] = jnp.zeros((16, D), BF)

    @pl.when(jnp.logical_not(has_above))
    def _():
        k.back[0:16, :] = jnp.zeros((16, D), BF)
        k.fall[...] = jnp.zeros((16, D), BF)
        k.edges[96:128, :] = jnp.zeros((32, D), BF)

    barrier = pltpu.get_barrier_semaphore()

    def greet(to_lat, to_lon):
        pl.semaphore_signal(barrier, inc=1, device_id=(to_lat, to_lon), device_id_type=MESH)

    far, sibling = lax.rem(lat + 2, 4), lat // 2 * 2 + (1 - lat % 2)

    def greet_lon(i, carry):
        greet(lat, lax.rem(lon + i, 32))
        greet(far, lax.rem(lon + i, 32))
        return carry

    lax.fori_loop(1, 32, greet_lon, 0)
    for s in range(1, 4):
        greet(lax.rem(lat + s, 4), lon)
    greet(above, west)
    greet(below, east)

    def send(source, target, sem, to_lat, to_lon):
        return pltpu.make_async_remote_copy(
            src_ref=source,
            dst_ref=target,
            send_sem=k.send_sem.at[sem],
            recv_sem=k.recv_sem.at[sem],
            device_id=(to_lat, to_lon),
            device_id_type=MESH,
        )

    def start(copies):
        for copy in copies:
            copy.start()

    def wait_received(copies):
        for copy in copies:
            copy.wait_recv()

    def await_bytes(ref, sem):
        pltpu.make_async_copy(ref, ref, sem).wait()

    fill_constants(k)
    fill_routes(k, lon)

    load_x.wait()
    for quad in range(4):
        cells_split(k, quad)
    up = one_where(iota((32, 32), 1) == iota((32, 32), 0) + 1)
    top = one_where((iota((16, 32), 0) == 15) & (iota((16, 32), 1) == 0))
    left, right = k.means[0].astype(BF), k.means[1].astype(BF)
    k.car_send[0:32, :] = nn(up, left).astype(BF)
    k.car_send[32:48, :] = nn(top, left).astype(BF)
    k.car_send[48:64, :] = nn(top, right).astype(BF)
    own = nn(up, right)
    pl.semaphore_wait(barrier, 67)
    carriers_west = send(k.car_send.at[0:32], k.car_beside, 0, lat, west)
    carriers_corner = send(k.car_send.at[32:48], k.car_corner, 1, above, west)
    carriers_above = send(k.car_send.at[48:64], k.car_below, 2, above, lon)
    cells = []
    for first in range(0, 496, 64):
        last = min(first + 64, 496)
        cells.append(
            send(
                k.away.at[16 + first : 16 + last],
                k.x.at[512 + first : 512 + last],
                20 + first // 64,
                lat,
                west,
            )
        )
    cells_corner = send(k.away.at[0:16], k.x.at[1008:1024], 5, above, west)
    cells_above = send(k.rise, k.x.at[496:512], 6, above, lon)
    carriers_west.start()

    @pl.when(has_above)
    def _():
        carriers_corner.start()
        carriers_above.start()
        cells_above.start()

    start(cells[0:2])
    load_w.wait()
    cells_project(k, 0)
    start(cells[2:3])
    load_g.wait()
    load_we.wait()
    loop(2, cells_sensitivity, k)

    carriers_west.wait_recv()

    @pl.when(has_below)
    def _():
        carriers_corner.wait_recv()
        carriers_above.wait_recv()

    lower = jnp.concatenate([jnp.zeros((16, D), F32), k.car_below[...].astype(F32)], axis=0)
    own = (own + lower).astype(BF)
    lower = jnp.concatenate([jnp.zeros((16, D), F32), k.car_corner[...].astype(F32)], axis=0)
    beside = (k.car_beside[...].astype(F32) + lower).astype(BF)

    def exchange(index, slabs, direction):
        out, back = k.slab_out.at[index], k.slab_in.at[index]
        out[...] = slabs
        back[0] = slabs[0]

        def step(i, carry):
            to_lon = lax.rem(lon + direction * i + 32, 32)
            pltpu.make_async_remote_copy(
                src_ref=out.at[i],
                dst_ref=back.at[i],
                send_sem=k.slab_send_sem.at[index],
                recv_sem=k.slab_recv_sem.at[index],
                device_id=(lat, to_lon),
                device_id_type=MESH,
            ).start()
            return carry

        def far_step(i, carry):
            to_lon = lax.rem(lon + direction * i + 32, 32)
            pltpu.make_async_remote_copy(
                src_ref=out.at[i],
                dst_ref=k.slab_far.at[index // 2, i],
                send_sem=k.far_send_sem.at[index // 2],
                recv_sem=k.far_recv_sem.at[index // 2],
                device_id=(far, to_lon),
                device_id_type=MESH,
            ).start()
            return carry

        lax.fori_loop(1, 32, step, 0)
        if direction == 1:
            lax.fori_loop(0, 32, far_step, 0)

    def group_gather(index, ref, sem):
        ref[0:64, :] = unpack_owner(k, exchanged(index))
        await_bytes(k.slab_far.at[index // 2], k.far_recv_sem.at[index // 2])
        ref[64:128, :] = unpack_owner(k, k.slab_far.at[index // 2])
        copy = send(ref.at[0:128], ref.at[128:256], sem, sibling, lon)
        copy.start()
        return copy

    def exchanged(index):
        await_bytes(k.slab_in.at[index, 1:32], k.slab_recv_sem.at[index])
        return k.slab_in.at[index]

    exchange(0, pack_home(k, jnp.concatenate([own, beside], axis=0)), 1)

    @pl.when(has_below)
    def _():
        cells_above.wait_recv()

    start(cells[3:4])
    cells_project(k, 1)
    start(cells[4:6])
    loop_from(2, 4, cells_sensitivity, k)
    k.gsum[...] = nn(k.gather[...], k.g[...])
    wait_received(cells[0:4])
    cells_project(k, 2)

    members = group_gather(0, k.car, 7)
    start(cells[6:7])
    cells_attend(k, 0)
    load_cw.wait()
    load_cwe.wait()
    members.wait_recv()
    exchange(1, pack_owner(k, group_forward(k)), -1)

    start(cells[7:8])

    @pl.when(has_above)
    def _():
        cells_corner.start()

    cells_attend(k, 1)
    wait_received(cells[4:8])

    @pl.when(has_below)
    def _():
        cells_corner.wait_recv()

    cells_project(k, 3)
    loop_from(2, 4, cells_attend, k)

    k.cn[...] = unpack_home(k, exchanged(1))
    carriers_project(k)
    loop(4, windows_finish, k)
    exchange(2, pack_home(k, carriers_back(k)), 1)

    grads = []
    for first in range(0, 496, 64):
        last = min(first + 64, 496)
        grads.append(
            send(
                k.dx.at[512 + first : 512 + last],
                k.back.at[16 + first : 16 + last],
                28 + first // 64,
                lat,
                east,
            )
        )
    grads_corner = send(k.dx.at[1008:1024], k.back.at[0:16], 15, below, east)
    grads_below = send(k.dx.at[496:512], k.fall, 16, below, lon)
    sensitivities = send(k.cgrad.at[0:128], k.cgrad.at[128:256], 8, sibling, lon)

    def back_step(quad, carry):
        @pl.when(quad == 2)
        def _():
            group_others(k)
            group_gather(2, k.cgrad, 8)
            start(grads[2:3])

        @pl.when(quad == 3)
        def _():
            start(grads[3:5])
            sensitivities.wait_recv()
            exchange(3, pack_owner(k, group_back(k)), -1)
            start(grads[5:6])

        cells_back(k, quad)
        cells_gradient(k, 512 + quad * 128, 128)
        for piece, at in ((0, 0), (1, 1), (6, 3)):
            pl.when(quad == at)(grads[piece].start)
        return carry

    lax.fori_loop(0, 4, back_step, 0)

    def left_step(i, carry):
        cells_gradient(k, 256 - 256 * i, 256)
        pl.when(i == 0)(grads[7].start)

        @pl.when((i == 0) & has_below)
        def _():
            grads_corner.start()
            grads_below.start()

        return carry

    lax.fori_loop(0, 2, left_step, 0)
    k.edges[0:64, :] = unpack_home(k, exchanged(3))
    pool_east = send(k.edges.at[32:64], k.edges.at[64:96], 17, lat, east)
    pool_corner = send(k.edges.at[48:64], k.edges.at[96:112], 18, below, east)
    pool_below = send(k.edges.at[16:32], k.edges.at[112:128], 19, below, lon)
    pool_east.start()

    @pl.when(has_below)
    def _():
        pool_corner.start()
        pool_below.start()

    loop(4, cells_result, k)
    store_out = pltpu.make_async_copy(k.xraw, k.result_hbm, k.load_sem.at[6])
    store_out.start()
    stores = [
        pltpu.make_async_copy(k.dx.at[0:496], k.grads_hbm.at[528:1024], k.store_sem.at[0]),
        pltpu.make_async_copy(k.back, k.grads_hbm.at[0:512], k.store_sem.at[1]),
        pltpu.make_async_copy(k.fall, k.grads_hbm.at[512:528], k.store_sem.at[2]),
        pltpu.make_async_copy(k.edges, k.edges_hbm, k.store_sem.at[3]),
    ]
    stores[0].start()

    wait_received(grads)

    @pl.when(has_above)
    def _():
        grads_corner.wait_recv()
        grads_below.wait_recv()

    start(stores[1:3])
    pool_east.wait_recv()

    @pl.when(has_above)
    def _():
        pool_corner.wait_recv()
        pool_below.wait_recv()

    stores[3].start()

    for copy in [carriers_west, members, sensitivities, pool_east] + cells + grads:
        copy.wait_send()

    @pl.when(has_above)
    def _():
        for copy in (carriers_corner, carriers_above, cells_corner, cells_above):
            copy.wait_send()

    @pl.when(has_below)
    def _():
        for copy in (grads_corner, grads_below, pool_corner, pool_below):
            copy.wait_send()

    for index in range(4):
        await_bytes(k.slab_out.at[index, 1:32], k.slab_send_sem.at[index])
    for index in range(2):
        await_bytes(k.slab_out.at[0], k.far_send_sem.at[index])
    store_out.wait()
    for store in stores:
        store.wait()


def loop(count, step, k):
    loop_from(0, count, step, k)


def loop_from(first, last, step, k):
    lax.fori_loop(first, last, lambda i, _: (step(k, i), 0)[1], 0)


SCRATCH = {
    "heads": ((256, 256), BF),
    "carrier_heads": ((256, D), BF),
    "same": ((256, 256), BF),
    "spread": ((1024, 64), BF),
    "gather": ((64, 1024), BF),
    "split": ((256, 256), BF),
    "unpack": ((384, HALF), BF),
    "routes": ((384, HALF), BF),
    "gain": ((1, D), F32),
    "cgain": ((1, D), F32),
    "temper": ((1, D), F32),
    "ctemper": ((1, D), F32),
    "xraw": ((1024, D), BF),
    "graw": ((1024, D), BF),
    "w": ((D, 3 * D), BF),
    "we": ((D, D), BF),
    "cw": ((D, 3 * D), BF),
    "cwe": ((D, D), BF),
    "x": ((1024, D), BF),
    "g": ((1024, D), BF),
    "away": ((HALF, D), BF),
    "rise": ((16, D), BF),
    "means": ((2, 32, D), F32),
    "car_send": ((64, D), BF),
    "car_beside": ((32, D), BF),
    "car_corner": ((16, D), BF),
    "car_below": ((16, D), BF),
    "slab_out": ((4, 32, 16, 128), BF),
    "slab_in": ((4, 32, 16, 128), BF),
    "slab_far": ((2, 32, 16, 128), BF),
    "car": ((256, D), BF),
    "cgrad": ((256, D), BF),
    "cn": ((64, D), BF),
    "edges": ((128, D), BF),
    "back": ((HALF, D), BF),
    "fall": ((16, D), BF),
    "dx": ((1024, D), BF),
    "q": ((1024, D), BF),
    "k": ((1024, D), BF),
    "v": ((1024, D), BF),
    "do": ((1024, D), BF),
    "o": ((1024, D), BF),
    "t": ((1024, D), BF),
    "p": ((1024, D), BF),
    "sq": ((1024, D), F32),
    "sk": ((1024, D), F32),
    "op": ((1024, D), F32),
    "lp": ((1024, D), F32),
    "kcb": ((1024, D), BF),
    "vcb": ((1024, D), BF),
    "kc": ((64, D), BF),
    "vc": ((64, D), BF),
    "skc": ((64, D), F32),
    "dqkv": ((1024, 3 * D), BF),
    "cq": ((256, D), BF),
    "ck": ((256, D), BF),
    "cv": ((256, D), BF),
    "chid": ((256, D), BF),
    "crows": ((3, 256, 256), BF),
    "ccolumns": ((3, 256, 256), BF),
    "cg": ((1024, 256), BF),
    "gsum": ((64, D), F32),
    "csq": ((64, D), F32),
    "csk": ((64, D), F32),
    "cl": ((256, D), F32),
    "co": ((256, D), F32),
}
SEMAPHORES = {
    "load_sem": 7,
    "store_sem": 4,
    "send_sem": 36,
    "recv_sem": 36,
    "far_send_sem": 2,
    "far_recv_sem": 2,
    "slab_send_sem": 4,
    "slab_recv_sem": 4,
}
INPUTS = (
    "x_hbm",
    "g_hbm",
    "w_hbm",
    "we_hbm",
    "cw_hbm",
    "cwe_hbm",
    "gains",
    "cgains",
    "place",
    "tempers",
    "ctempers",
)


def per_device(x, g, gain, w, we, tempers, cgain, cw, cwe, ctempers, place):
    names = INPUTS + ("result_hbm", "grads_hbm", "edges_hbm") + tuple(SCRATCH) + tuple(SEMAPHORES)

    def kernel(*refs):
        body(types.SimpleNamespace(**dict(zip(names, refs))))

    anywhere = pl.BlockSpec(memory_space=pl.ANY)
    vmem = pl.BlockSpec(memory_space=pltpu.VMEM)
    smem = pl.BlockSpec(memory_space=pltpu.SMEM)
    result, grads, edges = pl.pallas_call(
        kernel,
        out_shape=[jax.ShapeDtypeStruct((rows, D), BF) for rows in (1024, 1024, 128)],
        in_specs=[anywhere] * 6 + [vmem] * 3 + [smem] * 2,
        out_specs=[anywhere] * 3,
        scratch_shapes=[pltpu.VMEM(shape, kind) for shape, kind in SCRATCH.values()]
        + [pltpu.SemaphoreType.DMA((count,)) for count in SEMAPHORES.values()],
        compiler_params=pltpu.CompilerParams(
            collective_id=0, has_side_effects=True, vmem_limit_bytes=62 * 1024 * 1024
        ),
        name="block",
    )(
        x.reshape(1024, D),
        g.reshape(1024, D),
        w,
        we,
        cw,
        cwe,
        gain,
        cgain,
        place.T,
        tempers,
        ctempers,
    )
    halves = pl.BlockSpec((2, 256, D), lambda step: (0, step, 0))
    cells = pl.BlockSpec((512, D), lambda step: (step, 0))
    out, field = pl.pallas_call(
        assemble,
        grid=(2,),
        out_shape=[jax.ShapeDtypeStruct((1024, D), BF)] * 2,
        in_specs=[halves, halves, pl.BlockSpec((128, D), lambda step: (0, 0))],
        out_specs=[cells, cells],
        name="assemble",
    )(result.reshape(2, HALF, D), grads.reshape(2, HALF, D), edges)
    return out.reshape(128, 8, D), field.reshape(128, 8, D)


def solution(mesh):
    placed = (P("lat", "lon", None),) * 2 + (P(),) * 8 + (P("lat", "lon"),)
    return jax.shard_map(
        per_device,
        mesh=mesh,
        in_specs=placed,
        out_specs=(P("lat", "lon", None),) * 2,
        check_vma=False,
    )
```

profile of v0, /device:TPU:1, one launch (start us, length us, event | category | flops | bytes accessed | tf_op | source)
XLA Modules:
  0.0 104.2 jit_solution(7680999816784045463)
XLA Ops:
  0.6 98.8 %block.1 = (bf16[1024,768]{1,0:T(8,128)(2,1)}, bf16[1024,768]{1,0:T(8,128)(2,1)}, bf16[128,768]{1,0:T(8,128)(2,1)}) custom-call(bf16[1024,768]{1,0:T(8,128)(2,1)} %bitcast.7, bf16[1024,768]{1,0:T(8,128)(2,1)} %bitcast.8, bf16[768,2304]{1,0:T(8,128)(2,1)} %refs_2_.1, bf16[768,768]{1,0:T(8,128)(2,1)} %refs_3_.1, bf16[768,2304]{1,0:T(8,128)(2,1)} %refs_4_.1, ...), custom_call_target="tpu_custom_call" | custom-call | tf_op jit(solution)/shard_map/block/pallas_call | solution.py:872
  99.5 4.7 %assemble.1 = (bf16[1024,768]{1,0:T(8,128)(2,1)}, bf16[1024,768]{1,0:T(8,128)(2,1)}) custom-call(bf16[2,512,768]{2,1,0:T(8,128)(2,1)} %bitcast.9, bf16[2,512,768]{2,1,0:T(8,128)(2,1)} %bitcast.10, bf16[128,768]{1,0:T(8,128)(2,1)} %get-tuple-element.9.edges), custom_call_target="tpu_custom_call" | custom-call | tf_op jit(solution)/shard_map/assemble/pallas_call | solution.py:898
where the time goes:
time: 104 us
  Pallas kernels  104 us (100%)
    pallas_call x1, Pallas kernels, per_device(): pl.pallas_call(kernel, out_shape=[jax.ShapeDtypeStruct((rows, D), BF) for...  98.8 us
    pallas_call x1, Pallas kernels, per_device(): pl.pallas_call(assemble, grid=(2,), out_shape=[jax.ShapeDtypeStruct((1024...  4.75 us

commit v1 on v0

--- a/solution.py
+++ b/solution.py
@@ -634,6 +634,7 @@
         cells_corner.start()
 
     cells_attend(k, 1)
+    group_others(k)
     wait_received(cells[4:8])
 
     @pl.when(has_below)
@@ -667,7 +668,6 @@
     def back_step(quad, carry):
         @pl.when(quad == 2)
         def _():
-            group_others(k)
             group_gather(2, k.cgrad, 8)
             start(grads[2:3])
 

time: 104 us -> 101 us (0.971)
  Pallas kernels: 104 us -> 101 us
    pallas_call x1, Pallas kernels: 98.8 us -> 95.8 us  [per_device(): pl.pallas_call(kernel, out_shape=[jax.ShapeDtypeStruct((rows, D), BF) for...]
where the time goes in v1:
time: 101 us
  Pallas kernels  101 us (100%)
    pallas_call x1, Pallas kernels, per_device(): pl.pallas_call(kernel, out_shape=[jax.ShapeDtypeStruct((rows, D), BF) for...  95.8 us
    pallas_call x1, Pallas kernels, per_device(): pl.pallas_call(assemble, grid=(2,), out_shape=[jax.ShapeDtypeStruct((1024...  4.75 us

profile of v1, /device:TPU:1, one launch (start us, length us, event | category | flops | bytes accessed | tf_op | source)
XLA Modules:
  0.0 101.1 jit_solution(5569302410815616813)
XLA Ops:
  0.6 95.8 %block.1 = (bf16[1024,768]{1,0:T(8,128)(2,1)}, bf16[1024,768]{1,0:T(8,128)(2,1)}, bf16[128,768]{1,0:T(8,128)(2,1)}) custom-call(bf16[1024,768]{1,0:T(8,128)(2,1)} %bitcast.7, bf16[1024,768]{1,0:T(8,128)(2,1)} %bitcast.8, bf16[768,2304]{1,0:T(8,128)(2,1)} %refs_2_.1, bf16[768,768]{1,0:T(8,128)(2,1)} %refs_3_.1, bf16[768,2304]{1,0:T(8,128)(2,1)} %refs_4_.1, ...), custom_call_target="tpu_custom_call" | custom-call | tf_op jit(solution)/shard_map/block/pallas_call | solution.py:872
  96.4 4.7 %assemble.1 = (bf16[1024,768]{1,0:T(8,128)(2,1)}, bf16[1024,768]{1,0:T(8,128)(2,1)}) custom-call(bf16[2,512,768]{2,1,0:T(8,128)(2,1)} %bitcast.9, bf16[2,512,768]{2,1,0:T(8,128)(2,1)} %bitcast.10, bf16[128,768]{1,0:T(8,128)(2,1)} %get-tuple-element.9.edges), custom_call_target="tpu_custom_call" | custom-call | tf_op jit(solution)/shard_map/assemble/pallas_call | solution.py:898
